TPU v7x, 256 devices: a whole 4x4x8 slice. The times are simulated.
256 devices in a mesh: shape: 4 (over y), space: 64 (over x, z, core).
Axes of the slice: x: 4, y: 4, z: 8, core: 2. Of those that a mesh axis runs over, the one named last changes fastest.
Arguments:
- features: bfloat16 [4, 128, 512, 128], P('shape', 'space'), may hold values from -45 to 45
- gain_one: float32 [128], replicated, may hold values from 0.1 to 1.9
- weight_one: bfloat16 [7, 128, 128], replicated, may hold values from -0.1875 to 0.1875
- gain_two: float32 [128], replicated, may hold values from 0.1 to 1.9
- weight_two: bfloat16 [7, 128, 128], replicated, may hold values from -0.1875 to 0.1875
- live: int32 [4, 128], P('shape', 'space'), may hold values from 0 to 1, as said below
- send_index: int32 [4, 64, 64, 1], P('shape', 'space'), may hold values from -1 to 11, as said below
- recv_index: int32 [4, 128, 6], P('shape', 'space'), may hold values from -1 to 63, as said below
- cotangent: bfloat16 [4, 128, 512, 128], P('shape', 'space'), may hold values from -6 to 6
Outputs:
- output: bfloat16 [4, 128, 512, 128], P('shape', 'space')
- grad_features: bfloat16 [4, 128, 512, 128], P('shape', 'space')
- grad_weight_one: float32 [7, 128, 128], replicated
- grad_weight_two: float32 [7, 128, 128], replicated
- grad_gain_one: float32 [128], replicated
- grad_gain_two: float32 [128], replicated
Inputs may be any that keep to these rules, and one draw needn't show every extreme that they name: The live slots of each device are its first ones, at least 1 of them; in every shape one device has both slots live and another only 1. `recv_index`: -1 where the face has no neighbour slab, always so on slots that are not live; else a position r of the device's receive buffer of 64 slabs, r being the sending device (one slab per sender). No two faces of one device share a position; on every device the slot from some sender is in use; slot 0 of every device has all six faces. send_index[s, d, e, c] is -1 where slot c from device d to device e is unused, else 6 b + f for a live slot b of device d, f being the opposite of the face of the brick of e that reads that slot; it agrees with recv_index.
All inputs are finite; a program needn't handle non-finite values.
Results may differ from a plain program's by a relative error of at most 0.014.
Values may be sent and summed in bfloat16 or wider, within the bound.
A program may use at most 64 MiB of HBM per device.

v0:
```python
import math
import jax
import jax.numpy as jnp
from jax import lax
from jax.sharding import PartitionSpec as P

EDGE = 8
OFFSETS = ((0, 0, 0), (-1, 0, 0), (1, 0, 0), (0, -1, 0), (0, 1, 0), (0, 0, -1), (0, 0, 1))
norm_epsilon = 1e-05


def pre_act(values, gain):
    row_mean = jnp.mean(values, axis=-1, keepdims=True)
    centered = values - row_mean
    variance = jnp.mean(centered * centered, axis=-1, keepdims=True)
    return jax.nn.silu(centered * lax.rsqrt(variance + norm_epsilon) * gain)


def pre_back(brick_cube, gain, upstream):
    outputs, pullback = jax.vjp(pre_act, brick_cube.astype(jnp.float32), gain)
    return pullback(upstream)


def face_slabs(brick_cube):
    brick_count = brick_cube.shape[0]
    edge_len = brick_cube.shape[1]
    last_layer = edge_len - 1
    face_list = [
        brick_cube[:, 0],
        brick_cube[:, last_layer],
        brick_cube[:, :, 0],
        brick_cube[:, :, last_layer],
        brick_cube[:, :, :, 0],
        brick_cube[:, :, :, last_layer],
    ]
    return jnp.stack(
        [
            face_part.reshape(brick_count, edge_len * edge_len, brick_cube.shape[-1])
            for face_part in face_list
        ],
        axis=1,
    )


def pad_cube(brick_cube, halo_slabs):
    brick_count = brick_cube.shape[0]
    edge_len = brick_cube.shape[1]
    channels = brick_cube.shape[-1]
    slab_grid = halo_slabs.reshape(brick_count, 6, edge_len, edge_len, channels)
    far_side = edge_len + 1
    inside = slice(1, far_side)
    padded = jnp.pad(brick_cube, ((0, 0), (1, 1), (1, 1), (1, 1), (0, 0)))
    padded = padded.at[:, 0, inside, inside].set(slab_grid[:, 0])
    padded = padded.at[:, far_side, inside, inside].set(slab_grid[:, 1])
    padded = padded.at[:, inside, 0, inside].set(slab_grid[:, 2])
    padded = padded.at[:, inside, far_side, inside].set(slab_grid[:, 3])
    padded = padded.at[:, inside, inside, 0].set(slab_grid[:, 4])
    padded = padded.at[:, inside, inside, far_side].set(slab_grid[:, 5])
    return padded


def add_faces(volume, face_terms):
    brick_count = volume.shape[0]
    edge_len = volume.shape[1]
    channels = volume.shape[-1]
    term_grid = face_terms.reshape(brick_count, 6, edge_len, edge_len, channels)
    last_layer = edge_len - 1
    volume = volume.at[:, 0].add(term_grid[:, 0])
    volume = volume.at[:, last_layer].add(term_grid[:, 1])
    volume = volume.at[:, :, 0].add(term_grid[:, 2])
    volume = volume.at[:, :, last_layer].add(term_grid[:, 3])
    volume = volume.at[:, :, :, 0].add(term_grid[:, 4])
    volume = volume.at[:, :, :, last_layer].add(term_grid[:, 5])
    return volume


def shifted(padded, tap_index):
    step_i, step_j, step_k = OFFSETS[tap_index]
    edge_len = padded.shape[1] - 2
    window = padded[
        :,
        1 + step_i : 1 + step_i + edge_len,
        1 + step_j : 1 + step_j + edge_len,
        1 + step_k : 1 + step_k + edge_len,
    ]
    return window.reshape(-1, padded.shape[-1])


def convolve(padded, weight):
    running = jnp.dot(shifted(padded, 0), weight[0], preferred_element_type=jnp.float32)
    for tap_index in range(1, len(OFFSETS)):
        running = running + jnp.dot(
            shifted(padded, tap_index), weight[tap_index], preferred_element_type=jnp.float32
        )
    return running


def conv_back(padded, grad_rows, weight):
    brick_count = padded.shape[0]
    edge_len = padded.shape[1] - 2
    channels = padded.shape[-1]
    weight_grad = jnp.stack(
        [
            lax.dot_general(
                shifted(padded, tap_index),
                grad_rows,
                (((0,), (0,)), ((), ())),
                preferred_element_type=jnp.float32,
            )
            for tap_index in range(len(OFFSETS))
        ]
    )
    spread = jnp.zeros(padded.shape, jnp.float32)
    for tap_index in range(len(OFFSETS)):
        step_i, step_j, step_k = OFFSETS[tap_index]
        tap_term = lax.dot_general(
            grad_rows,
            weight[tap_index],
            (((1,), (1,)), ((), ())),
            preferred_element_type=jnp.float32,
        )
        tap_term = tap_term.reshape(brick_count, edge_len, edge_len, edge_len, channels)
        spread = spread.at[
            :,
            1 + step_i : 1 + step_i + edge_len,
            1 + step_j : 1 + step_j + edge_len,
            1 + step_k : 1 + step_k + edge_len,
        ].add(tap_term)
    far_side = edge_len + 1
    inside = slice(1, far_side)
    interior = spread[:, inside, inside, inside]
    face_list = [
        spread[:, 0, inside, inside],
        spread[:, far_side, inside, inside],
        spread[:, inside, 0, inside],
        spread[:, inside, far_side, inside],
        spread[:, inside, inside, 0],
        spread[:, inside, inside, far_side],
    ]
    halo_grad = jnp.stack(
        [face_part.reshape(brick_count, edge_len * edge_len, channels) for face_part in face_list],
        axis=1,
    ).astype(jnp.bfloat16)
    return (weight_grad, interior, halo_grad)


def trade_faces(brick_cube, send_pick, recv_pick, peer_count, slot_count):
    face_rows = face_slabs(brick_cube)
    flat_rows = face_rows.reshape(send_pick.shape[1], -1)
    outgoing = jnp.dot(send_pick, flat_rows, preferred_element_type=jnp.float32).astype(
        jnp.bfloat16
    )
    incoming = lax.all_to_all(
        outgoing.reshape(peer_count, slot_count, -1),
        "space",
        split_axis=0,
        concat_axis=0,
        tiled=True,
    )
    halo_slabs = jnp.dot(
        recv_pick, incoming.reshape(peer_count * slot_count, -1), preferred_element_type=jnp.float32
    ).astype(jnp.bfloat16)
    return halo_slabs.reshape(face_rows.shape)


def return_slabs(halo_grad, send_pick, recv_pick, peer_count, slot_count):
    flat_rows = halo_grad.reshape(recv_pick.shape[0], -1)
    outgoing = lax.dot_general(
        recv_pick, flat_rows, (((0,), (0,)), ((), ())), preferred_element_type=jnp.float32
    ).astype(jnp.bfloat16)
    incoming = lax.all_to_all(
        outgoing.reshape(peer_count, slot_count, -1),
        "space",
        split_axis=0,
        concat_axis=0,
        tiled=True,
    )
    summed = lax.dot_general(
        send_pick,
        incoming.reshape(peer_count * slot_count, -1),
        (((0,), (0,)), ((), ())),
        preferred_element_type=jnp.float32,
    )
    return summed.reshape(halo_grad.shape)


def forward_conv(brick_cube, weight, send_pick, recv_pick, peer_count, slot_count):
    halo_slabs = trade_faces(brick_cube, send_pick, recv_pick, peer_count, slot_count)
    padded = pad_cube(brick_cube, halo_slabs)
    result = convolve(padded, weight).reshape(brick_cube.shape)
    return (result, padded)


def shards(
    features, gain_one, weight_one, gain_two, weight_two, live, send_index, recv_index, cotangent
):
    brick_count = features.shape[1]
    channels = features.shape[3]
    edge_len = EDGE
    peer_count = lax.axis_size("space")
    slot_count = send_index.shape[3]
    cube_shape = (brick_count, edge_len, edge_len, edge_len, channels)
    cubes_in = features.reshape(cube_shape)
    cot_cube = cotangent.reshape(cube_shape)
    alive_rows = (live.reshape(brick_count) > 0)[:, None, None, None, None]
    send_codes = send_index.reshape(peer_count * slot_count)
    places = recv_index.reshape(brick_count * 6)
    send_pick = (
        send_codes[:, None] == jnp.arange(brick_count * 6, dtype=jnp.int32)[None, :]
    ).astype(jnp.bfloat16)
    recv_pick = (
        places[:, None] == jnp.arange(peer_count * slot_count, dtype=jnp.int32)[None, :]
    ).astype(jnp.bfloat16)
    acts_one = pre_act(cubes_in.astype(jnp.float32), gain_one).astype(jnp.bfloat16)
    conv_one, padded_one = forward_conv(
        acts_one, weight_one, send_pick, recv_pick, peer_count, slot_count
    )
    hidden = conv_one.astype(jnp.bfloat16)
    acts_two = pre_act(hidden.astype(jnp.float32), gain_two).astype(jnp.bfloat16)
    conv_two, padded_two = forward_conv(
        acts_two, weight_two, send_pick, recv_pick, peer_count, slot_count
    )
    output = jnp.where(
        alive_rows, cubes_in.astype(jnp.float32) + conv_two, jnp.zeros(conv_two.shape, jnp.float32)
    ).astype(jnp.bfloat16)
    grad_rows = jnp.where(alive_rows, cot_cube, jnp.zeros_like(cot_cube))
    weight_grad_two, interior_two, halo_grad_two = conv_back(
        padded_two, grad_rows.reshape(-1, channels), weight_two
    )
    returned_two = return_slabs(halo_grad_two, send_pick, recv_pick, peer_count, slot_count)
    grad_hidden, gain_grad_two = pre_back(hidden, gain_two, add_faces(interior_two, returned_two))
    grad_hidden = grad_hidden.astype(jnp.bfloat16)
    weight_grad_one, interior_one, halo_grad_one = conv_back(
        padded_one, grad_hidden.reshape(-1, channels), weight_one
    )
    returned_one = return_slabs(halo_grad_one, send_pick, recv_pick, peer_count, slot_count)
    grad_input, gain_grad_one = pre_back(cubes_in, gain_one, add_faces(interior_one, returned_one))
    direct = jnp.where(
        alive_rows, cot_cube.astype(jnp.float32), jnp.zeros(grad_input.shape, jnp.float32)
    )
    grad_features = (direct + grad_input).astype(jnp.bfloat16)
    weight_sum_one, weight_sum_two, gain_sum_one, gain_sum_two = lax.psum(
        (weight_grad_one, weight_grad_two, gain_grad_one, gain_grad_two), ("shape", "space")
    )
    total_rows = (
        features.shape[0] * lax.axis_size("shape") * brick_count * peer_count * features.shape[2]
    )
    grad_scale = 1.0 / math.sqrt(total_rows)
    return (
        output.reshape(features.shape),
        grad_features.reshape(features.shape),
        weight_sum_one * grad_scale,
        weight_sum_two * grad_scale,
        gain_sum_one * grad_scale,
        gain_sum_two * grad_scale,
    )


def solution(mesh):
    in_specs = (
        P("shape", "space", None, None),
        P(),
        P(),
        P(),
        P(),
        P("shape", "space"),
        P("shape", "space", None, None),
        P("shape", "space", None),
        P("shape", "space", None, None),
    )
    out_specs = (
        P("shape", "space", None, None),
        P("shape", "space", None, None),
        P(),
        P(),
        P(),
        P(),
    )
    return jax.shard_map(shards, mesh=mesh, in_specs=in_specs, out_specs=out_specs, check_vma=False)
```

profile of v0, /device:TPU:4, one launch (start us, length us, event | category | flops | bytes accessed | tf_op | source)
XLA Modules:
  0.0 569.2 jit_solution(17979509776324319021)
XLA Ops:
  16.4 12.4 %all-to-all-start = ((bf16[64,2,4096]{2,1,0:T(2,128)(2,1)}), bf16[64,2,4096]{2,1,0:T(2,128)(2,1)}, u32[]{:S(2)}, u32[]{:S(2)}) async-start(bf16[64,2,4096]{2,1,0:T(2,128)(2,1)} %reshape.1985), calls=%async_computation | async-start | bytes 2097152 | tf_op jit(solution)/shard_map/all_to_all | solution.py:153
  31.3 2.7 scatter-add.89
  34.3 2.7 scatter-add.90
  37.2 2.7 scatter-add.91
  40.1 2.7 scatter-add.94
  43.3 2.7 scatter-add.96
  54.3 3.3 reduce.80
  57.6 2.6 reshape.1989
  60.2 11.2 %all-to-all-start.2 = ((bf16[64,2,4096]{2,1,0:T(2,128)(2,1)}), bf16[64,2,4096]{2,1,0:T(2,128)(2,1)}, u32[]{:S(2)}, u32[]{:S(2)}) async-start(bf16[64,2,4096]{2,1,0:T(2,128)(2,1)} %reshape.1989), calls=%async_computation.2 | async-start | bytes 2097152 | tf_op jit(solution)/shard_map/all_to_all | solution.py:171
  71.4 7.5 %reshape.1986 = bf16[64,1,8192]{2,1,0:T(2,128)(2,1)} reshape(bf16[64,2,4096]{2,1,0:T(2,128)(2,1)} %all-to-all-done) | data formatting | bytes 2097152
  78.9 2.8 convolution_convert_fusion.5
  88.9 8.9 %all-to-all-done.2 = bf16[64,2,4096]{2,1,0:T(2,128)(2,1)} async-done(((bf16[64,2,4096]{2,1,0:T(2,128)(2,1)}), bf16[64,2,4096]{2,1,0:T(2,128)(2,1)}, u32[]{:S(2)}, u32[]{:S(2)}) %all-to-all-start.2) | async-done | bytes 1048608 | tf_op jit(solution)/shard_map/all_to_all | solution.py:171
  97.8 7.5 %reshape.1990 = bf16[64,1,8192]{2,1,0:T(2,128)(2,1)} reshape(bf16[64,2,4096]{2,1,0:T(2,128)(2,1)} %all-to-all-done.2) | data formatting | bytes 2097152
  105.3 2.7 copy.213
  115.6 2.7 scatter-add.110
  118.6 2.9 scatter-add.111
  121.7 2.7 scatter-add.114
  124.6 2.7 scatter-add.115
  127.8 2.7 scatter-add.119
  135.1 2.6 reshape.1991
  137.7 8.3 %all-to-all-start.3 = ((bf16[64,2,4096]{2,1,0:T(2,128)(2,1)}), bf16[64,2,4096]{2,1,0:T(2,128)(2,1)}, u32[]{:S(2)}, u32[]{:S(2)}) async-start(bf16[64,2,4096]{2,1,0:T(2,128)(2,1)} %reshape.1991), calls=%async_computation.3 | async-start | bytes 2097152 | tf_op jit(solution)/shard_map/all_to_all | solution.py:171
  152.0 3.3 reduce.82
  155.4 2.6 reshape.1987
  164.6 7.9 %all-to-all-done.3 = bf16[64,2,4096]{2,1,0:T(2,128)(2,1)} async-done(((bf16[64,2,4096]{2,1,0:T(2,128)(2,1)}), bf16[64,2,4096]{2,1,0:T(2,128)(2,1)}, u32[]{:S(2)}, u32[]{:S(2)}) %all-to-all-start.3) | async-done | bytes 1048608 | tf_op jit(solution)/shard_map/all_to_all | solution.py:171
  172.6 8.3 %all-to-all-start.1 = ((bf16[64,2,4096]{2,1,0:T(2,128)(2,1)}), bf16[64,2,4096]{2,1,0:T(2,128)(2,1)}, u32[]{:S(2)}, u32[]{:S(2)}) async-start(bf16[64,2,4096]{2,1,0:T(2,128)(2,1)} %reshape.1987), calls=%async_computation.1 | async-start | bytes 2097152 | tf_op jit(solution)/shard_map/all_to_all | solution.py:153
  180.9 2.2 fusion.15
  183.1 7.5 %reshape.1992 = bf16[64,1,8192]{2,1,0:T(2,128)(2,1)} reshape(bf16[64,2,4096]{2,1,0:T(2,128)(2,1)} %all-to-all-done.3) | data formatting | bytes 2097152
  190.6 2.7 copy.212
  197.5 10.0 %all-to-all-done.1 = bf16[64,2,4096]{2,1,0:T(2,128)(2,1)} async-done(((bf16[64,2,4096]{2,1,0:T(2,128)(2,1)}), bf16[64,2,4096]{2,1,0:T(2,128)(2,1)}, u32[]{:S(2)}, u32[]{:S(2)}) %all-to-all-start.1) | async-done | bytes 1048608 | tf_op jit(solution)/shard_map/all_to_all | solution.py:153
  207.5 6.5 %reshape.1988 = bf16[64,1,8192]{2,1,0:T(2,128)(2,1)S(1)} reshape(bf16[64,2,4096]{2,1,0:T(2,128)(2,1)} %all-to-all-done.1) | data formatting | bytes 2097152
  232.3 76.4 %all-reduce.4 = (f32[128]{0:T(128)S(1)}, f32[128]{0:T(128)S(1)}) all-reduce(f32[128]{0:T(128)S(1)} %get-tuple-element.462, f32[128]{0:T(128)S(1)} %get-tuple-element.464), channel_id=1, replica_groups=mesh['shape'=4,'space'=64] {'shape','space'}, use_global_device_ids=true, to_apply=%region_11.12 | all-reduce | flops 256 | bytes 2048 | tf_op jit(solution)/shard_map/psum | solution.py:242
  310.6 249.3 %all-reduce.8.cloned.1.call-done = (f32[7,128,128]{2,1,0:T(8,128)}, f32[7,128,128]{2,1,0:T(8,128)}) async-done(((f32[7,128,128]{2,1,0:T(8,128)}, f32[7,128,128]{2,1,0:T(8,128)}), (f32[7,128,128]{2,1,0:T(8,128)}, f32[7,128,128]{2,1,0:T(8,128)})) %all-reduce.8.cloned.1.call-update) | async-done | bytes 917520 | tf_op jit(solution)/shard_map/psum | solution.py:242
  (244 shorter events, 79.9 us)
Async XLA Ops:
  9.7 2.7 copy-start.4
  9.8 2.3 copy-start.21
  9.8 2.5 copy-start.6
  9.9 2.5 copy-start.26
  16.4 12.6 %copy-start.30 = (s32[1,2]{1,0:T(1,128)S(1)}, s32[1,2]{1,0:T(1,128)}, u32[]{:S(2)}) copy-start(s32[1,2]{1,0:T(1,128)} %param.90) | copy-start | bytes 28
  16.4 12.6 %copy-start.10 = (bf16[1,2,512,128]{3,2,1,0:T(8,128)(2,1)S(1)}, bf16[1,2,512,128]{3,2,1,0:T(8,128)(2,1)}, u32[]{:S(2)}) copy-start(bf16[1,2,512,128]{3,2,1,0:T(8,128)(2,1)} %param.93) | copy-start | bytes 786436
  16.4 43.8 %all-to-all-start = ((bf16[64,2,4096]{2,1,0:T(2,128)(2,1)}), bf16[64,2,4096]{2,1,0:T(2,128)(2,1)}, u32[]{:S(2)}, u32[]{:S(2)}) async-start(bf16[64,2,4096]{2,1,0:T(2,128)(2,1)} %reshape.1985), calls=%async_computation | async-start | bytes 2097152 | tf_op jit(solution)/shard_map/all_to_all | solution.py:153
  31.1 2.9 copy-start.17
  46.7 1.1 copy-start.29
  46.7 5.7 %copy-start.23 = (bf16[2,8,8,1,128]{4,3,2,1,0:T(2,128)(2,1)S(1)}, bf16[2,8,8,1,128]{4,3,2,1,0:T(2,128)(2,1)}, u32[]{:S(2)}) copy-start(bf16[2,8,8,1,128]{4,3,2,1,0:T(2,128)(2,1)} %slice.2143) | copy-start | bytes 98308
  60.2 37.6 %all-to-all-start.2 = ((bf16[64,2,4096]{2,1,0:T(2,128)(2,1)}), bf16[64,2,4096]{2,1,0:T(2,128)(2,1)}, u32[]{:S(2)}, u32[]{:S(2)}) async-start(bf16[64,2,4096]{2,1,0:T(2,128)(2,1)} %reshape.1989), calls=%async_computation.2 | async-start | bytes 2097152 | tf_op jit(solution)/shard_map/all_to_all | solution.py:171
  85.4 1.2 copy-start.15
  88.4 24.1 %copy-start.13 = (f32[2,8,8,8]{3,2,1,0:T(8,128)}, f32[2,8,8,8]{3,2,1,0:T(8,128)S(1)}, u32[]{:S(2)}) copy-start(f32[2,8,8,8]{3,2,1,0:T(8,128)S(1)} %div.59) | copy-start | bytes 12292
  88.9 23.7 %copy-start.14 = (f32[2,8,8,8]{3,2,1,0:T(8,128)}, f32[2,8,8,8]{3,2,1,0:T(8,128)S(1)}, u32[]{:S(2)}) copy-start(f32[2,8,8,8]{3,2,1,0:T(8,128)S(1)} %rsqrt.23) | copy-start | bytes 12292
  108.3 3.8 copy-start.28
  113.1 1.9 copy-start.16
  137.7 34.8 %all-to-all-start.3 = ((bf16[64,2,4096]{2,1,0:T(2,128)(2,1)}), bf16[64,2,4096]{2,1,0:T(2,128)(2,1)}, u32[]{:S(2)}, u32[]{:S(2)}) async-start(bf16[64,2,4096]{2,1,0:T(2,128)(2,1)} %reshape.1991), calls=%async_computation.3 | async-start | bytes 2097152 | tf_op jit(solution)/shard_map/all_to_all | solution.py:171
  146.0 2.1 copy-start.25
  146.0 2.8 copy-start.24
  158.0 2.0 copy-start.1
  172.6 34.9 %all-to-all-start.1 = ((bf16[64,2,4096]{2,1,0:T(2,128)(2,1)}), bf16[64,2,4096]{2,1,0:T(2,128)(2,1)}, u32[]{:S(2)}, u32[]{:S(2)}) async-start(bf16[64,2,4096]{2,1,0:T(2,128)(2,1)} %reshape.1987), calls=%async_computation.1 | async-start | bytes 2097152 | tf_op jit(solution)/shard_map/all_to_all | solution.py:153
  180.9 379.1 %all-reduce.8.cloned.1.call-start = ((), (), s32[]{:S(2)}) async-start(), calls=%async_computation.4 | async-start | bytes 1835008 | tf_op jit(solution)/shard_map/psum | solution.py:242
  218.8 1.3 copy-start.11
  225.6 1.0 copy-start.7
  225.7 1.0 copy-start.27
  226.6 2.9 copy-start.18
  226.7 3.0 copy-start.9
  228.1 1.3 copy-start.19
  228.1 1.7 copy-start.8
  230.8 78.5 %copy-start.12 = (bf16[1,2,512,128]{3,2,1,0:T(8,128)(2,1)S(1)}, bf16[1,2,512,128]{3,2,1,0:T(8,128)(2,1)}, u32[]{:S(2)}) copy-start(bf16[1,2,512,128]{3,2,1,0:T(8,128)(2,1)} %param.93) | copy-start | bytes 786436
  230.8 78.5 %copy-start.20 = (f32[2,8,8,8]{3,2,1,0:T(8,128)S(1)}, f32[2,8,8,8]{3,2,1,0:T(8,128)}, u32[]{:S(2)}) copy-start(f32[2,8,8,8]{3,2,1,0:T(8,128)} %copy-done.19) | copy-start | bytes 12292
  230.8 78.5 %copy-start.22 = (f32[2,8,8,8]{3,2,1,0:T(8,128)S(1)}, f32[2,8,8,8]{3,2,1,0:T(8,128)}, u32[]{:S(2)}) copy-start(f32[2,8,8,8]{3,2,1,0:T(8,128)} %negate_multiply_fusion) | copy-start | bytes 12292
  (4 other events, 4.0 us)
Sparse Core Ops, SparseCore 0:
  308.8 251.0 all-reduce.7
where the time goes:
time: 579 us; the launch traced here: 569 us
  waiting for transfers between devices  276 us (48%)
  local copies, waits for them, and re-layouts  101 us (17%)
  blocking collectives  76.4 us (13%)
  starting transfers between devices  40.2 us (7%)
  matrix products  32.7 us (6%)
  other arithmetic  27.2 us (5%)
  between operations  15.6 us (3%)
    psum x1, waiting for transfers between devices, shards(): lax.psum((weight_grad_one, weight_grad_two, gain_grad_one, gain_grad_two)...  249 us
    psum x1, blocking collectives, shards(): lax.psum((weight_grad_one, weight_grad_two, gain_grad_one, gain_grad_two)...  76.4 us
    unnamed x106, local copies, waits for them, and re-layouts  53.6 us
    scatter-add x12, local copies, waits for them, and re-layouts, conv_back(): spread = spread.at[:, 1 + step_i:1 + step_i + edge_len, 1 + step_j:1 + st...  27.4 us
    all_to_all x2, starting transfers between devices, trade_faces(): lax.all_to_all(outgoing.reshape(peer_count, slot_count, -1), 'space', spl...  20.7 us
    all_to_all x2, starting transfers between devices, return_slabs(): lax.all_to_all(outgoing.reshape(peer_count, slot_count, -1), 'space', spl...  19.4 us
    all_to_all x2, waiting for transfers between devices, return_slabs(): lax.all_to_all(outgoing.reshape(peer_count, slot_count, -1), 'space', spl...  16.8 us
    dot_general x14, matrix products, conv_back(): lax.dot_general(shifted(padded, tap_index), grad_rows, (((0,), (0,)), (()...  15.3 us
  transfers between devices with their start and end apart: 5, of which 4 were waited for; matrix products, arithmetic and copies ran while one was open for 15% of the time, Pallas kernels for 0%

commit v1 on v0

--- a/solution.py
+++ b/solution.py
@@ -240,7 +240,7 @@
     )
     grad_features = (direct + grad_input).astype(jnp.bfloat16)
     weight_sum_one, weight_sum_two, gain_sum_one, gain_sum_two = lax.psum(
-        (weight_grad_one, weight_grad_two, gain_grad_one, gain_grad_two), ("shape", "space")
+        lax.psum((weight_grad_one, weight_grad_two, gain_grad_one, gain_grad_two), "shape"), "space"
     )
     total_rows = (
         features.shape[0] * lax.axis_size("shape") * brick_count * peer_count * features.shape[2]

time: 579 us -> 617 us (1.066)
  blocking collectives: 76.4 us -> 116 us
    psum x1, waiting for transfers between devices: 249 us -> 58.5 us  [shards(): lax.psum((weight_grad_one, weight_grad_two, gain_grad_one, gain_grad_two)...]
    psum x0 -> x1, waiting for transfers between devices: none -> 188 us  [shards(): lax.psum(lax.psum((weight_grad_one, weight_grad_two, gain_grad_one, gain_...]
    psum x0 -> x1, blocking collectives: none -> 105 us  [shards(): lax.psum(lax.psum((weight_grad_one, weight_grad_two, gain_grad_one, gain_...]
    psum x1, blocking collectives: 76.4 us -> 10.7 us  [shards(): lax.psum((weight_grad_one, weight_grad_two, gain_grad_one, gain_grad_two)...]
    unnamed x106 -> x104, local copies, waits for them, and re-layouts: 53.6 us -> 53.9 us
  transfers between devices with their start and end apart: 5 -> 6, of which waited for: 4 -> 5; matrix products, arithmetic and copies ran while one was open for 15% -> 14% of each run, Pallas kernels for 0% -> 0%
where the time goes in v1:
time: 617 us; the launch traced here: 606 us
  waiting for transfers between devices  273 us (44%)
  blocking collectives  116 us (19%)
  local copies, waits for them, and re-layouts  101 us (16%)
  starting transfers between devices  40.2 us (7%)
  matrix products  33.6 us (5%)
  other arithmetic  27.1 us (4%)
  between operations  15.5 us (3%)
    psum x1, waiting for transfers between devices, shards(): lax.psum(lax.psum((weight_grad_one, weight_grad_two, gain_grad_one, gain_...  188 us
    psum x1, blocking collectives, shards(): lax.psum(lax.psum((weight_grad_one, weight_grad_two, gain_grad_one, gain_...  105 us
    psum x1, waiting for transfers between devices, shards(): lax.psum((weight_grad_one, weight_grad_two, gain_grad_one, gain_grad_two)...  58.5 us
    unnamed x104, local copies, waits for them, and re-layouts  53.9 us
    scatter-add x12, local copies, waits for them, and re-layouts, conv_back(): spread = spread.at[:, 1 + step_i:1 + step_i + edge_len, 1 + step_j:1 + st...  27.4 us
    all_to_all x2, starting transfers between devices, trade_faces(): lax.all_to_all(outgoing.reshape(peer_count, slot_count, -1), 'space', spl...  20.7 us
    all_to_all x2, starting transfers between devices, return_slabs(): lax.all_to_all(outgoing.reshape(peer_count, slot_count, -1), 'space', spl...  19.5 us
    all_to_all x2, waiting for transfers between devices, return_slabs(): lax.all_to_all(outgoing.reshape(peer_count, slot_count, -1), 'space', spl...  16.9 us
  transfers between devices with their start and end apart: 6, of which 5 were waited for; matrix products, arithmetic and copies ran while one was open for 14% of the time, Pallas kernels for 0%

profile of v1, /device:TPU:4, one launch (start us, length us, event | category | flops | bytes accessed | tf_op | source)
XLA Modules:
  0.0 606.4 jit_solution(16481577145022564467)
XLA Ops:
  16.4 12.4 %all-to-all-start = ((bf16[64,2,4096]{2,1,0:T(2,128)(2,1)}), bf16[64,2,4096]{2,1,0:T(2,128)(2,1)}, u32[]{:S(2)}, u32[]{:S(2)}) async-start(bf16[64,2,4096]{2,1,0:T(2,128)(2,1)} %reshape.1985), calls=%async_computation | async-start | bytes 2097152 | tf_op jit(solution)/shard_map/all_to_all | solution.py:153
  31.3 2.7 scatter-add.89
  34.2 2.7 scatter-add.90
  37.2 2.7 scatter-add.91
  40.1 2.7 scatter-add.94
  43.3 2.7 scatter-add.96
  54.2 3.3 reduce.80
  57.6 2.6 reshape.1989
  60.2 11.2 %all-to-all-start.2 = ((bf16[64,2,4096]{2,1,0:T(2,128)(2,1)}), bf16[64,2,4096]{2,1,0:T(2,128)(2,1)}, u32[]{:S(2)}, u32[]{:S(2)}) async-start(bf16[64,2,4096]{2,1,0:T(2,128)(2,1)} %reshape.1989), calls=%async_computation.2 | async-start | bytes 2097152 | tf_op jit(solution)/shard_map/all_to_all | solution.py:171
  71.4 7.5 %reshape.1986 = bf16[64,1,8192]{2,1,0:T(2,128)(2,1)} reshape(bf16[64,2,4096]{2,1,0:T(2,128)(2,1)} %all-to-all-done) | data formatting | bytes 2097152
  78.9 2.8 convolution_convert_fusion.5
  88.8 8.9 %all-to-all-done.2 = bf16[64,2,4096]{2,1,0:T(2,128)(2,1)} async-done(((bf16[64,2,4096]{2,1,0:T(2,128)(2,1)}), bf16[64,2,4096]{2,1,0:T(2,128)(2,1)}, u32[]{:S(2)}, u32[]{:S(2)}) %all-to-all-start.2) | async-done | bytes 1048608 | tf_op jit(solution)/shard_map/all_to_all | solution.py:171
  97.7 7.5 %reshape.1990 = bf16[64,1,8192]{2,1,0:T(2,128)(2,1)} reshape(bf16[64,2,4096]{2,1,0:T(2,128)(2,1)} %all-to-all-done.2) | data formatting | bytes 2097152
  105.2 2.7 copy.213
  115.6 2.7 scatter-add.110
  118.5 2.9 scatter-add.111
  121.6 2.7 scatter-add.114
  124.5 2.7 scatter-add.115
  127.7 2.7 scatter-add.119
  137.7 8.3 %all-to-all-start.3 = ((bf16[64,2,4096]{2,1,0:T(2,128)(2,1)}), bf16[64,2,4096]{2,1,0:T(2,128)(2,1)}, u32[]{:S(2)}, u32[]{:S(2)}) async-start(bf16[64,2,4096]{2,1,0:T(2,128)(2,1)} %reshape.1991), calls=%async_computation.3 | async-start | bytes 2097152 | tf_op jit(solution)/shard_map/all_to_all | solution.py:171
  152.0 3.3 reduce.82
  155.3 2.6 reshape.1987
  164.6 7.9 %all-to-all-done.3 = bf16[64,2,4096]{2,1,0:T(2,128)(2,1)} async-done(((bf16[64,2,4096]{2,1,0:T(2,128)(2,1)}), bf16[64,2,4096]{2,1,0:T(2,128)(2,1)}, u32[]{:S(2)}, u32[]{:S(2)}) %all-to-all-start.3) | async-done | bytes 1048608 | tf_op jit(solution)/shard_map/all_to_all | solution.py:171
  172.5 8.3 %all-to-all-start.1 = ((bf16[64,2,4096]{2,1,0:T(2,128)(2,1)}), bf16[64,2,4096]{2,1,0:T(2,128)(2,1)}, u32[]{:S(2)}, u32[]{:S(2)}) async-start(bf16[64,2,4096]{2,1,0:T(2,128)(2,1)} %reshape.1987), calls=%async_computation.1 | async-start | bytes 2097152 | tf_op jit(solution)/shard_map/all_to_all | solution.py:153
  183.0 7.5 %reshape.1992 = bf16[64,1,8192]{2,1,0:T(2,128)(2,1)} reshape(bf16[64,2,4096]{2,1,0:T(2,128)(2,1)} %all-to-all-done.3) | data formatting | bytes 2097152
  190.5 2.7 copy.212
  197.4 10.0 %all-to-all-done.1 = bf16[64,2,4096]{2,1,0:T(2,128)(2,1)} async-done(((bf16[64,2,4096]{2,1,0:T(2,128)(2,1)}), bf16[64,2,4096]{2,1,0:T(2,128)(2,1)}, u32[]{:S(2)}, u32[]{:S(2)}) %all-to-all-start.1) | async-done | bytes 1048608 | tf_op jit(solution)/shard_map/all_to_all | solution.py:153
  207.4 6.5 %reshape.1988 = bf16[64,1,8192]{2,1,0:T(2,128)(2,1)S(1)} reshape(bf16[64,2,4096]{2,1,0:T(2,128)(2,1)} %all-to-all-done.1) | data formatting | bytes 2097152
  229.5 10.7 %all-reduce.6 = (f32[128]{0:T(128)S(1)}, f32[128]{0:T(128)S(1)}) all-reduce(f32[128]{0:T(128)S(1)} %get-tuple-element.462, f32[128]{0:T(128)S(1)} %get-tuple-element.464), channel_id=1, replica_groups=mesh['shape'=4,'space'=64] {'shape'}, use_global_device_ids=true, to_apply=%region_13.14 | all-reduce | flops 256 | bytes 2048 | tf_op jit(solution)/shard_map/psum | solution.py:243
  240.3 104.8 %all-reduce.4 = (f32[128]{0:T(128)S(1)}, f32[128]{0:T(128)S(1)}) all-reduce(f32[128]{0:T(128)S(1)} %get-tuple-element.470, f32[128]{0:T(128)S(1)} %get-tuple-element.471), channel_id=1, replica_groups=mesh['shape'=4,'space'=64] {'space'}, use_global_device_ids=true, to_apply=%region_14.15 | all-reduce | flops 256 | bytes 2048 | tf_op jit(solution)/shard_map/psum | solution.py:242
  349.1 58.5 %all-reduce.13.cloned.1.call-done = (f32[7,128,128]{2,1,0:T(8,128)}, f32[7,128,128]{2,1,0:T(8,128)}) async-done(((f32[7,128,128]{2,1,0:T(8,128)}, f32[7,128,128]{2,1,0:T(8,128)}), (f32[7,128,128]{2,1,0:T(8,128)}, f32[7,128,128]{2,1,0:T(8,128)})) %all-reduce.13.cloned.1.call-update) | async-done | bytes 917520 | tf_op jit(solution)/shard_map/psum | solution.py:243
  409.6 187.6 %all-reduce.11.cloned.1.call-done = (f32[7,128,128]{2,1,0:T(8,128)}, f32[7,128,128]{2,1,0:T(8,128)}) async-done(((f32[7,128,128]{2,1,0:T(8,128)}, f32[7,128,128]{2,1,0:T(8,128)}), (f32[7,128,128]{2,1,0:T(8,128)}, f32[7,128,128]{2,1,0:T(8,128)})) %all-reduce.11.cloned.1.call-update) | async-done | bytes 917520 | tf_op jit(solution)/shard_map/psum | solution.py:242
  (246 shorter events, 86.0 us)
Async XLA Ops:
  9.7 2.7 copy-start.4
  9.8 2.3 copy-start.20
  9.8 2.5 copy-start.6
  9.9 2.5 copy-start.25
  16.4 12.6 %copy-start.29 = (s32[1,2]{1,0:T(1,128)S(1)}, s32[1,2]{1,0:T(1,128)}, u32[]{:S(2)}) copy-start(s32[1,2]{1,0:T(1,128)} %param.90) | copy-start | bytes 28
  16.4 12.6 %copy-start.9 = (bf16[1,2,512,128]{3,2,1,0:T(8,128)(2,1)S(1)}, bf16[1,2,512,128]{3,2,1,0:T(8,128)(2,1)}, u32[]{:S(2)}) copy-start(bf16[1,2,512,128]{3,2,1,0:T(8,128)(2,1)} %param.93) | copy-start | bytes 786436
  16.4 43.8 %all-to-all-start = ((bf16[64,2,4096]{2,1,0:T(2,128)(2,1)}), bf16[64,2,4096]{2,1,0:T(2,128)(2,1)}, u32[]{:S(2)}, u32[]{:S(2)}) async-start(bf16[64,2,4096]{2,1,0:T(2,128)(2,1)} %reshape.1985), calls=%async_computation | async-start | bytes 2097152 | tf_op jit(solution)/shard_map/all_to_all | solution.py:153
  31.1 2.9 copy-start.16
  46.7 1.1 copy-start.28
  46.7 5.7 copy-start.22
  60.2 37.6 %all-to-all-start.2 = ((bf16[64,2,4096]{2,1,0:T(2,128)(2,1)}), bf16[64,2,4096]{2,1,0:T(2,128)(2,1)}, u32[]{:S(2)}, u32[]{:S(2)}) async-start(bf16[64,2,4096]{2,1,0:T(2,128)(2,1)} %reshape.1989), calls=%async_computation.2 | async-start | bytes 2097152 | tf_op jit(solution)/shard_map/all_to_all | solution.py:171
  85.3 1.2 copy-start.14
  88.3 24.2 %copy-start.12 = (f32[2,8,8,8]{3,2,1,0:T(8,128)}, f32[2,8,8,8]{3,2,1,0:T(8,128)S(1)}, u32[]{:S(2)}) copy-start(f32[2,8,8,8]{3,2,1,0:T(8,128)S(1)} %div.59) | copy-start | bytes 12292
  88.8 23.7 %copy-start.13 = (f32[2,8,8,8]{3,2,1,0:T(8,128)}, f32[2,8,8,8]{3,2,1,0:T(8,128)S(1)}, u32[]{:S(2)}) copy-start(f32[2,8,8,8]{3,2,1,0:T(8,128)S(1)} %rsqrt.23) | copy-start | bytes 12292
  108.3 3.8 copy-start.27
  113.0 1.9 copy-start.15
  137.7 34.9 %all-to-all-start.3 = ((bf16[64,2,4096]{2,1,0:T(2,128)(2,1)}), bf16[64,2,4096]{2,1,0:T(2,128)(2,1)}, u32[]{:S(2)}, u32[]{:S(2)}) async-start(bf16[64,2,4096]{2,1,0:T(2,128)(2,1)} %reshape.1991), calls=%async_computation.3 | async-start | bytes 2097152 | tf_op jit(solution)/shard_map/all_to_all | solution.py:171
  146.0 2.1 copy-start.24
  146.0 2.8 copy-start.23
  157.9 2.0 copy-start.1
  172.5 34.9 %all-to-all-start.1 = ((bf16[64,2,4096]{2,1,0:T(2,128)(2,1)}), bf16[64,2,4096]{2,1,0:T(2,128)(2,1)}, u32[]{:S(2)}, u32[]{:S(2)}) async-start(bf16[64,2,4096]{2,1,0:T(2,128)(2,1)} %reshape.1987), calls=%async_computation.1 | async-start | bytes 2097152 | tf_op jit(solution)/shard_map/all_to_all | solution.py:153
  180.8 226.9 %all-reduce.13.cloned.1.call-start = ((), (), s32[]{:S(2)}) async-start(), calls=%async_computation.5 | async-start | bytes 1835008 | tf_op jit(solution)/shard_map/psum | solution.py:243
  218.7 1.3 copy-start.10
  225.6 1.0 copy-start.5
  225.6 1.0 copy-start.7
  225.6 1.0 copy-start.26
  226.5 2.8 copy-start.17
  228.0 1.3 copy-start.18
  229.3 117.0 %copy-start.8 = (bf16[2,8,8,8,128]{4,3,2,1,0:T(8,128)(2,1)S(1)}, bf16[2,8,8,8,128]{4,3,2,1,0:T(8,128)(2,1)}, u32[]{:S(2)}) copy-start(bf16[2,8,8,8,128]{4,3,2,1,0:T(8,128)(2,1)} %get-tuple-element.480) | copy-start | bytes 786436
  345.1 252.1 %all-reduce.11.cloned.1.call-start = ((), (), s32[]{:S(2)}) async-start(), calls=%async_computation.4 | async-start | bytes 1835008 | tf_op jit(solution)/shard_map/psum | solution.py:242
  347.6 60.6 %copy-start.11 = (bf16[1,2,512,128]{3,2,1,0:T(8,128)(2,1)S(1)}, bf16[1,2,512,128]{3,2,1,0:T(8,128)(2,1)}, u32[]{:S(2)}) copy-start(bf16[1,2,512,128]{3,2,1,0:T(8,128)(2,1)} %param.93) | copy-start | bytes 786436
  347.6 60.6 %copy-start.19 = (f32[2,8,8,8]{3,2,1,0:T(8,128)S(1)}, f32[2,8,8,8]{3,2,1,0:T(8,128)}, u32[]{:S(2)}) copy-start(f32[2,8,8,8]{3,2,1,0:T(8,128)} %copy-done.18) | copy-start | bytes 12292
  (4 other events, 3.8 us)
Sparse Core Ops, SparseCore 0:
  345.2 62.4 all-reduce.12
  411.1 185.9 all-reduce.10
